TPU v7x, 32 devices: a whole 2x2x4 slice. The times are simulated.
32 devices in a mesh: cal: 2 (over x), gr: 4 (over y, core), gc: 4 (over z).
Axes of the slice: x: 2, y: 2, z: 4, core: 2. Of those that a mesh axis runs over, the one named last changes fastest.
Arguments:
- tokens: bfloat16 [512, 8192], P(('gr', 'gc'), 'cal'), may hold values from -12 to 12
- gate_weight: bfloat16 [8192, 28672], P(None, ('cal', 'gr', 'gc')), may hold values from -0.0625 to 0.0625
- up_weight: bfloat16 [8192, 28672], P(None, ('cal', 'gr', 'gc')), may hold values from -0.0625 to 0.0625
- hessian_slab: float32 [28672, 8192], P(('cal', 'gr'), 'gc'), may hold values from -1.2 to 1.2
- weight_error: float32 [512, 28672], P(None, ('cal', 'gr')), may hold values from -0.18 to 0.18
- slab_offset: int32 [1], replicated, may hold values from 0 to 20480
- token_count: int32 [1], replicated, may hold values from 512 to 1023
Outputs:
- new_slab: float32 [28672, 8192], P(('cal', 'gr'), 'gc')
- gradient: float32 [512, 8192], P(('cal', 'gr'), 'gc')
Inputs may be any that keep to these rules, and one draw needn't show every extreme that they name: The slab holds the Hessian's columns slab_offset[0] to slab_offset[0] + 8191.
All inputs are finite; a program needn't handle non-finite values.
Results may differ from a plain program's by a relative error of at most 0.0038.
Values may be sent and summed in bfloat16 or wider, within the bound.
A program may use at most 192 MiB of HBM per device.

v0:
```python
import jax
import jax.numpy as jnp
from jax import lax
from jax.sharding import PartitionSpec as P


def on_device(tokens, gate_weight, up_weight, hessian_slab, weight_error, slab_offset, token_count):
    token_rows = lax.all_gather(tokens, ("gr", "gc"), axis=0, tiled=True)
    token_piece = lax.all_gather(token_rows, "cal", axis=1, tiled=True)
    gate_pre = jnp.dot(token_piece, gate_weight, preferred_element_type=jnp.float32)
    up_pre = jnp.dot(token_piece, up_weight, preferred_element_type=jnp.float32)
    hidden = (jax.nn.silu(gate_pre) * up_pre).astype(jnp.bfloat16)
    row_panel = lax.all_gather(hidden, "gc", axis=1, tiled=True)
    panel_width = row_panel.shape[1]
    block_width = hessian_slab.shape[1]
    panel_index = lax.axis_index("cal") * lax.axis_size("gr") + lax.axis_index("gr")
    first_col = slab_offset[0] + lax.axis_index("gc") * block_width
    padded = jnp.pad(row_panel, ((0, 0), (block_width, block_width)))
    shifted = jnp.clip(
        first_col - panel_index * panel_width + block_width, 0, panel_width + block_width
    )
    own_share = lax.dynamic_slice_in_dim(padded, shifted, block_width, 1)
    window = lax.psum(own_share, ("cal", "gr")).astype(jnp.float32).astype(jnp.bfloat16)
    gram_block = lax.dot_general(
        row_panel, window, (((0,), (0,)), ((), ())), preferred_element_type=jnp.float32
    )
    new_slab = hessian_slab + gram_block / token_count[0].astype(jnp.float32)
    gradient = lax.psum_scatter(
        jnp.dot(
            weight_error,
            new_slab,
            precision=lax.Precision.HIGHEST,
            preferred_element_type=jnp.float32,
        ),
        ("cal", "gr"),
        scatter_dimension=0,
        tiled=True,
    )
    return (new_slab, gradient)


def solution(mesh):
    in_specs = (
        P(("gr", "gc"), "cal"),
        P(None, ("cal", "gr", "gc")),
        P(None, ("cal", "gr", "gc")),
        P(("cal", "gr"), "gc"),
        P(None, ("cal", "gr")),
        P(),
        P(),
    )
    out_specs = (P(("cal", "gr"), "gc"), P(("cal", "gr"), "gc"))
    return jax.shard_map(
        on_device, mesh=mesh, in_specs=in_specs, out_specs=out_specs, check_vma=False
    )
```

profile of v0, /device:TPU:0, one launch (start us, length us, event | category | flops | bytes accessed | tf_op | source)
XLA Modules:
  0.0 514.2 jit_solution(9602422390012987941)
XLA Ops:
  7.2 0.0 all-gather.4.cloned.1.call-start
  7.2 0.7 all-gather.4.cloned.1.call-update
  7.9 0.0 all-gather.6.cloned.1.call-start
  7.9 55.7 %all-gather.4.cloned.1.call-done = bf16[512,4096]{1,0:T(8,128)(2,1)} async-done(((bf16[32,4096]{1,0:T(8,128)(2,1)}), bf16[512,4096]{1,0:T(8,128)(2,1)}) %all-gather.4.cloned.1.call-update) | async-done | bytes 4194320 | tf_op jit(solution)/shard_map/all_gather | solution.py:8
  63.7 0.0 all-gather.6.cloned.1.call-update
  63.7 0.0 all-gather.8.cloned.1.call-start
  63.7 104.0 %all-gather.6.cloned.1.call-done = bf16[512,8192]{1,0:T(8,128)(2,1)} async-done(((bf16[512,4096]{1,0:T(8,128)(2,1)}), bf16[512,8192]{1,0:T(8,128)(2,1)}) %all-gather.6.cloned.1.call-update) | async-done | bytes 8388624 | tf_op jit(solution)/shard_map/all_gather | solution.py:9
  167.7 0.0 copy-start
  167.7 13.5 %fusion = f32[512,896]{1,0:T(8,128)S(1)} fusion(bf16[512,8192]{1,0:T(8,128)(2,1)} %all-gather.6.cloned.1.call-done, bf16[8192,896]{1,0:T(8,128)(2,1)} %param.8), kind=kOutput, calls=%fused_computation.4 | convolution fusion | flops 7516192768 | bytes 24903680 | tf_op jit(solution)/shard_map/dot_general | solution.py:10
  181.2 0.0 copy-done
  181.2 13.3 %multiply_convert_fusion = bf16[512,896]{1,0:T(8,128)(2,1)} fusion(f32[512,896]{1,0:T(8,128)S(1)} %fusion, bf16[512,8192]{1,0:T(8,128)(2,1)S(1)} %copy-done, bf16[8192,896]{1,0:T(8,128)(2,1)} %param.9), kind=kOutput, calls=%fused_computation.3 | convolution fusion | flops 7518945280 | bytes 25821184 | tf_op jit(solution)/shard_map/dot_general | solution.py:11
  194.5 0.0 all-gather.8.cloned.1.call-update
  194.6 0.0 all-reduce.3.cloned.1.call-start
  195.3 71.6 %all-gather.8.cloned.1.call-done = bf16[512,3584]{1,0:T(8,128)(2,1)} async-done(((bf16[512,896]{1,0:T(8,128)(2,1)}), bf16[512,3584]{1,0:T(8,128)(2,1)}) %all-gather.8.cloned.1.call-update) | async-done | bytes 3670032 | tf_op jit(solution)/shard_map/all_gather | solution.py:13
  266.8 0.0 slice-start
  266.8 2.3 pad_dynamic-slice_fusion
  269.1 0.0 all-reduce.3.cloned.1.call-update
  269.1 0.0 reduce-scatter.4.cloned.1.call-start
  269.8 60.7 %all-reduce.3.cloned.1.call-done = bf16[512,2048]{1,0:T(8,128)(2,1)} async-done(((bf16[512,2048]{1,0:T(8,128)(2,1)}), bf16[512,2048]{1,0:T(8,128)(2,1)}) %all-reduce.3.cloned.1.call-update) | async-done | bytes 2097168 | tf_op jit(solution)/shard_map/psum | solution.py:23
  330.6 0.0 slice-start.1
  330.6 25.2 %divide_add_fusion = f32[3584,2048]{1,0:T(8,128)} fusion(f32[3584,2048]{1,0:T(8,128)} %param.10, f32[]{:T(128)} %bitcast.1, bf16[512,3584]{1,0:T(8,128)(2,1)} %all-gather.8.cloned.1.call-done, bf16[512,2048]{1,0:T(8,128)(2,1)} %all-reduce.3.cloned.1.call-done), kind=kOutput, calls=%fused_computation | convolution fusion | flops 7530872832 | bytes 64487428 | tf_op jit(solution)/shard_map/dot_general | solution.py:24
  355.7 0.0 slice-done
  355.7 0.0 slice-done.1
  355.7 95.8 %convolution_bitcast_fusion = f32[512,2048]{0,1:T(8,128)} fusion(f32[3584,2048]{1,0:T(8,128)} %divide_add_fusion, f32[512,3584]{1,0:T(8,128)S(1)} %bitcast.15), kind=kOutput, calls=%fused_computation.2 | convolution fusion | flops 45097156608 | bytes 40894464 | tf_op jit(solution)/shard_map/dot_general | solution.py:29
  451.5 5.4 %copy.11 = f32[512,2048]{1,0:T(8,128)} copy(f32[512,2048]{0,1:T(8,128)} %convolution_bitcast_fusion) | data formatting | bytes 8388608
  457.0 0.0 reduce-scatter.4.cloned.1.call-update
  457.0 50.7 %reduce-scatter.4.cloned.1.call-done = f32[64,2048]{1,0:T(8,128)} async-done(((f32[512,2048]{1,0:T(8,128)}), f32[64,2048]{1,0:T(8,128)}) %reduce-scatter.4.cloned.1.call-update) | async-done | bytes 524304
  (1 shorter events, 0.0 us)
Async XLA Ops:
  7.2 56.5 %all-gather.4.cloned.1.call-start = ((), (), s32[]{:S(2)}) async-start(), calls=%async_computation.1 | async-start | bytes 4456448 | tf_op jit(solution)/shard_map/all_gather | solution.py:8
  7.9 159.8 %all-gather.6.cloned.1.call-start = ((), (), s32[]{:S(2)}) async-start(), calls=%async_computation.2 | async-start | bytes 12582912 | tf_op jit(solution)/shard_map/all_gather | solution.py:9
  63.7 203.1 %all-gather.8.cloned.1.call-start = ((), (), s32[]{:S(2)}) async-start(), calls=%async_computation.3 | async-start | bytes 4587520 | tf_op jit(solution)/shard_map/all_gather | solution.py:13
  167.7 13.5 %copy-start = (bf16[512,8192]{1,0:T(8,128)(2,1)S(1)}, bf16[512,8192]{1,0:T(8,128)(2,1)}, u32[]{:S(2)}) copy-start(bf16[512,8192]{1,0:T(8,128)(2,1)} %all-gather.6.cloned.1.call-done) | copy-start | bytes 25165828
  194.6 136.0 %all-reduce.3.cloned.1.call-start = ((), (), s32[]{:S(2)}) async-start(), calls=%async_computation.4 | async-start | bytes 4194304 | tf_op jit(solution)/shard_map/psum | solution.py:23
  266.8 88.9 %slice-start = ((s8[7340032]{0:T(1024)(128)(4,1)}), s8[3145728]{0:T(1024)(128)(4,1)S(1)}, s32[]{:S(2)}) async-start(s8[7340032]{0:T(1024)(128)(4,1)} %bitcast.14), calls=%async_computation.6 | async-start | bytes 6291456
  269.1 238.5 %reduce-scatter.4.cloned.1.call-start = ((), (), s32[]{:S(2)}) async-start(), calls=%async_computation.5 | async-start | bytes 4718592
  330.6 25.2 %slice-start.1 = ((s8[7340032]{0:T(1024)(128)(4,1)}), s8[4194304]{0:T(1024)(128)(4,1)S(1)}, s32[]{:S(2)}) async-start(s8[7340032]{0:T(1024)(128)(4,1)} %bitcast.14), calls=%async_computation.7 | async-start | bytes 8388608
Sparse Core Ops, SparseCore 0:
  10.2 53.3 all-gather.3
  65.2 102.4 all-gather.5
  194.7 72.1 all-gather.7
  270.5 60.0 all-reduce.2
  457.1 50.4 reduce-scatter.3
where the time goes:
time: 514 us
  waiting for transfers between devices  343 us (67%)
  matrix products  148 us (29%)
  between operations  15.1 us (3%)
  local copies, waits for them, and re-layouts  7.73 us (2%)
    all_gather x1, waiting for transfers between devices, on_device(): token_piece = lax.all_gather(token_rows, 'cal', axis=1, tiled=True)  104 us
    dot_general x1, matrix products, on_device(): jnp.dot(weight_error, new_slab, precision=lax.Precision.HIGHEST, preferre...  95.8 us
    all_gather x1, waiting for transfers between devices, on_device(): row_panel = lax.all_gather(hidden, 'gc', axis=1, tiled=True)  71.6 us
    psum x1, waiting for transfers between devices, on_device(): lax.psum(own_share, ('cal', 'gr')).astype(jnp.float32).astype(jnp.bfloat16)  60.7 us
    all_gather x1, waiting for transfers between devices, on_device(): token_rows = lax.all_gather(tokens, ('gr', 'gc'), axis=0, tiled=True)  55.7 us
    unnamed x6, waiting for transfers between devices  51.4 us
    dot_general x1, matrix products, on_device(): lax.dot_general(row_panel, window, (((0,), (0,)), ((), ())), preferred_el...  25.2 us
    dot_general x1, matrix products, on_device(): jnp.dot(token_piece, gate_weight, preferred_element_type=jnp.float32)  13.5 us
  transfers between devices with their start and end apart: 5, of which 5 were waited for; matrix products, arithmetic and copies ran while one was open for 0% of the time, Pallas kernels for 0%

commit v1 on v0

v1 whole, which is shorter than its diff:
```python
import functools

import jax
import jax.numpy as jnp
from jax import lax
from jax.experimental import pallas as pl
from jax.experimental.pallas import tpu as pltpu
from jax.sharding import PartitionSpec as P

MESH = pl.DeviceIdType.MESH
ANY = pl.BlockSpec(memory_space=pl.ANY)
VMEM = pl.BlockSpec(memory_space=pltpu.VMEM)


def place(dx, dy, dc):
    gr = lax.axis_index("gr")
    y, core = gr // 2, lax.rem(gr, 2)
    return (
        lax.rem(lax.axis_index("cal") + dx, 2),
        lax.rem(y + dy, 2) * 2 + lax.rem(core + dc, 2),
        lax.axis_index("gc"),
    )


def line_step(up):
    return (lax.axis_index("cal"), lax.axis_index("gr"), lax.axis_index("gc") + (1 if up else -1))


def greet(depth, partners, line):
    barrier = pltpu.get_barrier_semaphore()
    z = lax.axis_index("gc")
    for partner in partners:
        pl.semaphore_signal(barrier, inc=1, device_id=partner, device_id_type=MESH)
    if line:
        for up, there in ((True, z < depth - 1), (False, z > 0)):
            @pl.when(there)
            def _():
                pl.semaphore_signal(barrier, inc=1, device_id=line_step(up), device_id_type=MESH)
        both = jnp.where(z < depth - 1, 1, 0) + jnp.where(z > 0, 1, 0)
        pl.semaphore_wait(barrier, both + len(partners))
    else:
        pl.semaphore_wait(barrier, len(partners))


def line_events(depth):
    events = [(0, 0, None)]
    for d in range(1, depth):
        events += [(2 * d - 1, d, True), (2 * d, d, False)]
    return events


def here(depth, event):
    _, d, below = event
    z = lax.axis_index("gc")
    if below is None:
        return z >= 0, z
    if below:
        return z >= d, z - d
    return z + d < depth, z + d


def tokens_kernel(depth, x_ref, g_ref, own_sem, send, recv):
    rows, width = x_ref.shape
    z = lax.axis_index("gc")
    partners = [place(1, 0, 0), place(0, 1, 0), place(0, 0, 1)]
    x_next, y_next, sibling = partners
    greet(depth, partners, True)

    def block(where, origin, half=None):
        cal, gr, _ = where
        first = pl.multiple_of((gr * depth + origin) * rows, rows)
        count = rows
        if half is not None:
            count = rows // 2
            first = pl.multiple_of(first + half * count, count)
        return g_ref.at[pl.ds(first, count), pl.ds(pl.multiple_of(cal * width, width), width)]

    def copy(ref, target, kind, e, kind_there=None, e_there=None, src=None):
        return pltpu.make_async_remote_copy(
            src_ref=ref if src is None else src,
            dst_ref=ref,
            send_sem=send.at[kind, e],
            recv_sem=recv.at[kind, e if e_there is None else e_there],
            device_id=target,
            device_id_type=MESH,
        )

    mine = place(0, 0, 0)
    x_place, y_place, diag = place(1, 0, 0), place(0, 1, 0), place(1, 1, 0)
    events = line_events(depth)
    own = pltpu.make_async_copy(x_ref, block(mine, z), own_sem)
    own.start()

    def arrived(ref, kind, e):
        copy(ref, x_next, kind, e).wait_recv()

    def line_sends(event):
        e, d, below = event
        ok, origin = here(depth, event)
        src = x_ref if e == 0 else None
        out = []
        if below is not False:
            out.append((ok & (z < depth - 1), copy(block(mine, origin), line_step(True), 0, e, e_there=2 * d + 1, src=src)))
        if below is not True:
            out.append((ok & (z > 0), copy(block(mine, origin), line_step(False), 1, e, e_there=2 * d + 2, src=src)))
        return out

    def plane_sends(event):
        e = event[0]
        ok, origin = here(depth, event)
        src = x_ref if e == 0 else None
        ref = block(mine, origin)
        return [(ok, copy(ref, to, kind, e, src=src)) for kind, to in ((2, x_next), (3, y_next), (4, sibling))]

    def relay_sends(event):
        e = event[0]
        ok, origin = here(depth, event)
        return [
            (ok, copy(block(x_place, origin, 0), y_next, 5, e)),
            (ok, copy(block(x_place, origin), sibling, 7, e)),
        ], [
            (ok, copy(block(y_place, origin, 1), x_next, 6, e)),
            (ok, copy(block(y_place, origin), sibling, 8, e)),
        ]

    def diag_send(event):
        ok, origin = here(depth, event)
        return [(ok, copy(block(diag, origin), sibling, 9, event[0]))]

    def start(copies):
        for ok, c in copies:
            pl.when(ok)(c.start)

    count = len(events)
    for step in range(count + 2):
        if step < count:
            event = events[step]
            ok, origin = here(depth, event)
            if event[2] is not None:
                pl.when(ok)(lambda: arrived(block(mine, origin), 0 if event[2] else 1, event[0]))
            start(line_sends(event))
            start(plane_sends(event))
        if 1 <= step < count + 1:
            event = events[step - 1]
            ok, origin = here(depth, event)
            by_x, by_y = relay_sends(event)
            pl.when(ok)(lambda: arrived(block(x_place, origin), 2, event[0]))
            start(by_x)
            pl.when(ok)(lambda: arrived(block(y_place, origin), 3, event[0]))
            start(by_y)
        if step >= 2:
            event = events[step - 2]
            ok, origin = here(depth, event)
            pl.when(ok)(lambda: arrived(block(diag, origin, 0), 5, event[0]))
            pl.when(ok)(lambda: arrived(block(diag, origin, 1), 6, event[0]))
            start(diag_send(event))
    own.wait()
    for event in events:
        ok, origin = here(depth, event)
        for kind, at in ((4, (0, 0)), (7, (1, 0)), (8, (0, 1)), (9, (1, 1))):
            pl.when(ok)(lambda: arrived(block(place(*at, 1), origin), kind, event[0]))
        by_x, by_y = relay_sends(event)
        for there, c in line_sends(event) + plane_sends(event) + by_x + by_y + diag_send(event):
            pl.when(there)(c.wait_send)


def gather_tokens(tokens, depth):
    rows, width = tokens.shape
    events = 2 * depth + 1
    return pl.pallas_call(
        functools.partial(tokens_kernel, depth),
        out_shape=jax.ShapeDtypeStruct((rows * 4 * depth, width * 2), tokens.dtype),
        in_specs=[ANY],
        out_specs=ANY,
        scratch_shapes=[
            pltpu.SemaphoreType.DMA,
            pltpu.SemaphoreType.DMA((10, events)),
            pltpu.SemaphoreType.DMA((10, events)),
        ],
        compiler_params=pltpu.CompilerParams(collective_id=0, has_side_effects=True),
    )(tokens)


CHUNKS = 4
OTHERS = [(dx, dy, dc) for dx in (0, 1) for dy in (0, 1) for dc in (0, 1)][1:]


def flat(where):
    return where[0] * 4 + where[1]


def exchange(part_ref, got_ref, send, recv):
    rows = part_ref.shape[0] // 8
    copies = []
    for i, at in enumerate(OTHERS):
        to = place(*at)
        copies.append(
            pltpu.make_async_remote_copy(
                src_ref=part_ref.at[pl.ds(pl.multiple_of(flat(to) * rows, rows), rows), :],
                dst_ref=got_ref.at[i],
                send_sem=send.at[i],
                recv_sem=recv.at[i],
                device_id=to,
                device_id_type=MESH,
            )
        )
    return copies


def panel_kernel(depth, h_ref, part_ref, panel_ref, got_ref, own_sem, send, recv, psend, precv):
    total, width = h_ref.shape
    rows = total // CHUNKS
    z = lax.axis_index("gc")
    greet(depth, [place(*at) for at in OTHERS], True)
    events = line_events(depth)

    def block(origin, c):
        return panel_ref.at[pl.ds(c * rows, rows), pl.ds(pl.multiple_of(origin * width, width), width)]

    def copy(origin, c, up, e, e_there, src=None):
        return pltpu.make_async_remote_copy(
            src_ref=block(origin, c) if src is None else src,
            dst_ref=block(origin, c),
            send_sem=send.at[0 if up else 1, e, c],
            recv_sem=recv.at[0 if up else 1, e_there, c],
            device_id=line_step(up),
            device_id_type=MESH,
        )

    def sends(event, c):
        e, d, below = event
        ok, origin = here(depth, event)
        src = h_ref.at[pl.ds(c * rows, rows), :] if e == 0 else None
        out = []
        if below is not False:
            out.append((ok & (z < depth - 1), copy(origin, c, True, e, 2 * d + 1, src)))
        if below is not True:
            out.append((ok & (z > 0), copy(origin, c, False, e, 2 * d + 2, src)))
        return out

    own = pltpu.make_async_copy(h_ref, panel_ref.at[:, pl.ds(pl.multiple_of(z * width, width), width)], own_sem)
    for event in events:
        ok, origin = here(depth, event)
        for c in range(CHUNKS):
            if event[2] is not None:
                pl.when(ok)(copy(origin, c, event[2], 0, event[0]).wait_recv)
            for there, one in sends(event, c):
                pl.when(there)(one.start)
        if event[0] == 0:
            parts = exchange(part_ref, got_ref, psend, precv)
            for one in parts:
                one.start()
            own.start()
    own.wait()
    for one in parts:
        one.wait()
    for event in events:
        for c in range(CHUNKS):
            for there, one in sends(event, c):
                pl.when(there)(one.wait_send)


def gather_panel(hidden, part, depth):
    rows, width = hidden.shape
    events = 2 * depth + 1
    return pl.pallas_call(
        functools.partial(panel_kernel, depth),
        out_shape=(
            jax.ShapeDtypeStruct((rows, width * depth), hidden.dtype),
            jax.ShapeDtypeStruct((7, part.shape[0] // 8, part.shape[1]), part.dtype),
        ),
        in_specs=[ANY, ANY],
        out_specs=(ANY, ANY),
        scratch_shapes=[
            pltpu.SemaphoreType.DMA,
            pltpu.SemaphoreType.DMA((2, events, CHUNKS)),
            pltpu.SemaphoreType.DMA((2, events, CHUNKS)),
            pltpu.SemaphoreType.DMA((7,)),
            pltpu.SemaphoreType.DMA((7,)),
        ],
        compiler_params=pltpu.CompilerParams(collective_id=1, has_side_effects=True),
    )(hidden, part)


def window_kernel(share_ref, part_ref, window_ref, got_ref, land, send, recv, psend, precv):
    rows = share_ref.shape[0]
    half, quarter = rows // 2, rows // 4
    core = lax.rem(lax.axis_index("gr"), 2)
    x_next, y_next, sibling = place(1, 0, 0), place(0, 1, 0), place(0, 0, 1)
    greet(0, [place(*at) for at in OTHERS], False)

    def at(first, count):
        return pl.ds(pl.multiple_of(first, count), count)

    def copy(src, dst, i, to):
        return pltpu.make_async_remote_copy(
            src_ref=src, dst_ref=dst, send_sem=send.at[i], recv_sem=recv.at[i], device_id=to, device_id_type=MESH
        )

    def add(first, count, slot_first):
        mine = window_ref[at(first, count), :].astype(jnp.float32)
        other = land[pl.ds(slot_first, count), :].astype(jnp.float32)
        window_ref[at(first, count), :] = (mine + other).astype(window_ref.dtype)

    my, its = core * half, (1 - core) * half
    a, b = my, my + quarter
    first = copy(share_ref.at[at(its, half), :], land.at[pl.ds(0, half), :], 0, sibling)
    first.start()
    window_ref[at(my, half), :] = share_ref[at(my, half), :]
    first.wait_recv()
    add(my, half, 0)
    parts = exchange(part_ref, got_ref, psend, precv)
    s1 = copy(window_ref.at[at(a, quarter), :], land.at[pl.ds(half, quarter), :], 1, x_next)
    s2 = copy(window_ref.at[at(b, quarter), :], land.at[pl.ds(half + quarter, quarter), :], 2, y_next)
    s1.start()
    s2.start()
    for one in parts:
        one.start()
    s1.wait()
    add(a, quarter, half)
    s3 = copy(window_ref.at[at(a, quarter), :], land.at[pl.ds(2 * half, quarter), :], 3, y_next)
    s3.start()
    s2.wait()
    add(b, quarter, half + quarter)
    s4 = copy(window_ref.at[at(b, quarter), :], land.at[pl.ds(2 * half + quarter, quarter), :], 4, x_next)
    s4.start()
    s3.wait()
    add(a, quarter, 2 * half)
    s4.wait()
    add(b, quarter, 2 * half + quarter)
    last = copy(window_ref.at[at(my, half), :], window_ref.at[at(my, half), :], 5, sibling)
    last.start()
    first.wait_send()
    last.wait_send()
    copy(window_ref.at[at(its, half), :], window_ref.at[at(its, half), :], 5, sibling).wait_recv()
    for one in parts:
        one.wait()


def sum_window(share, part):
    rows, width = share.shape
    return pl.pallas_call(
        window_kernel,
        out_shape=(
            jax.ShapeDtypeStruct((rows, width), share.dtype),
            jax.ShapeDtypeStruct((7, part.shape[0] // 8, part.shape[1]), part.dtype),
        ),
        in_specs=[VMEM, ANY],
        out_specs=(VMEM, ANY),
        scratch_shapes=[
            pltpu.VMEM((3 * rows // 2, width), share.dtype),
            pltpu.SemaphoreType.DMA((6,)),
            pltpu.SemaphoreType.DMA((6,)),
            pltpu.SemaphoreType.DMA((7,)),
            pltpu.SemaphoreType.DMA((7,)),
        ],
        compiler_params=pltpu.CompilerParams(
            collective_id=2, has_side_effects=True, vmem_limit_bytes=24 * 1024 * 1024
        ),
    )(share, part)


def on_device(near, depth, tokens, gate_weight, up_weight, hessian_slab, weight_error, slab_offset, token_count):
    bf16, f32 = jnp.bfloat16, jnp.float32
    plane = ("cal", "gr")
    errors = weight_error.astype(bf16)
    plane_index = lax.axis_index("cal") * lax.axis_size("gr") + lax.axis_index("gr")

    def own_rows(part):
        count = part.shape[0] // (lax.axis_size("cal") * lax.axis_size("gr"))
        return lax.dynamic_slice_in_dim(part, plane_index * count, count, 0)

    if near:
        token_piece = gather_tokens(tokens, depth)
    else:
        token_rows = lax.all_gather(tokens, "cal", axis=1, tiled=True)
        token_piece = lax.all_gather(token_rows, ("gr", "gc"), axis=0, tiled=True)
    slab_part = jnp.dot(errors, hessian_slab.astype(bf16), preferred_element_type=f32)
    gate_pre = jnp.dot(token_piece, gate_weight, preferred_element_type=f32)
    up_pre = jnp.dot(token_piece, up_weight, preferred_element_type=f32)
    hidden = (jax.nn.silu(gate_pre) * up_pre).astype(bf16)
    if near:
        row_panel, slab_parts = gather_panel(hidden, slab_part, depth)
        slab_sum = own_rows(slab_part) + slab_parts.sum(0)
    else:
        row_panel = lax.all_gather(hidden, "gc", axis=1, tiled=True)
        slab_sum = lax.psum_scatter(slab_part, plane, scatter_dimension=0, tiled=True)
    panel_width = row_panel.shape[1]
    block_width = hessian_slab.shape[1]
    first_col = slab_offset[0] + lax.axis_index("gc") * block_width
    padded = jnp.pad(row_panel, ((0, 0), (block_width, block_width)))
    shifted = jnp.clip(
        first_col - plane_index * panel_width + block_width, 0, panel_width + block_width
    )
    own_share = lax.dynamic_slice_in_dim(padded, shifted, block_width, 1)
    mixed = lax.dot_general(errors, row_panel, (((1,), (1,)), ((), ())), preferred_element_type=f32)
    if near:
        window, mixed_parts = sum_window(own_share, mixed)
        mixed_sum = own_rows(mixed) + mixed_parts.sum(0)
    else:
        window = lax.psum(own_share, plane).astype(f32).astype(bf16)
        mixed_sum = lax.psum_scatter(mixed, plane, scatter_dimension=0, tiled=True)
    count = token_count[0].astype(f32)
    gram_block = lax.dot_general(
        row_panel, window, (((0,), (0,)), ((), ())), preferred_element_type=f32
    )
    new_slab = hessian_slab + gram_block / count
    gradient = slab_sum + jnp.dot(
        mixed_sum, window.astype(f32), precision=lax.Precision.HIGHEST, preferred_element_type=f32
    ) / count
    return (new_slab, gradient)


def solution(mesh):
    in_specs = (
        P(("gr", "gc"), "cal"),
        P(None, ("cal", "gr", "gc")),
        P(None, ("cal", "gr", "gc")),
        P(("cal", "gr"), "gc"),
        P(None, ("cal", "gr")),
        P(),
        P(),
    )
    out_specs = (P(("cal", "gr"), "gc"), P(("cal", "gr"), "gc"))
    near = mesh.shape["cal"] == 2 and mesh.shape["gr"] == 4
    return jax.shard_map(
        functools.partial(on_device, near, mesh.shape["gc"]),
        mesh=mesh, in_specs=in_specs, out_specs=out_specs, check_vma=False,
    )
```

time: 514 us -> 242 us (0.47)
  waiting for transfers between devices: 343 us -> 0 us
  Pallas kernels: 0 us -> 160 us
  matrix products: 148 us -> 74.2 us
  between operations: 15.1 us -> 2.05 us
  local copies, waits for them, and re-layouts: 7.73 us -> 1.91 us
    all_gather x3 -> x0, waiting for transfers between devices: 231 us -> none  [the longest x1 104 us: on_device(): token_piece = lax.all_gather(token_rows, 'cal', axis=1, tiled=True)]
    pallas_call x0 -> x3, Pallas kernels: none -> 160 us  [the longest x1 66.1 us: gather_panel(): pl.pallas_call(functools.partial(panel_kernel, depth), out_shape=(jax.Sha...]
    dot_general x3 -> x5, matrix products: 123 us -> 52.2 us  [the longest x1 16.7 us: on_device(): jnp.dot(errors, hessian_slab.astype(bf16), preferred_element_type=f32)]
    psum x1 -> x0, waiting for transfers between devices: 60.7 us -> none  [on_device(): lax.psum(own_share, ('cal', 'gr')).astype(jnp.float32).astype(jnp.bfloat16)]
    unnamed x6 -> x0, waiting for transfers between devices: 51.4 us -> none
  transfers between devices with their start and end apart: 5 -> 0, of which waited for: 5 -> 0; matrix products, arithmetic and copies ran while one was open for 0% -> 0% of each run, Pallas kernels for 0% -> 0%
where the time goes in v1:
time: 242 us
  Pallas kernels  160 us (66%)
  matrix products  74.2 us (31%)
  other arithmetic  4.34 us (2%)
    pallas_call x1, Pallas kernels, gather_panel(): pl.pallas_call(functools.partial(panel_kernel, depth), out_shape=(jax.Sha...  66.1 us
    pallas_call x1, Pallas kernels, gather_tokens(): pl.pallas_call(functools.partial(tokens_kernel, depth), out_shape=jax.Sha...  50.9 us
    pallas_call x1, Pallas kernels, sum_window(): pl.pallas_call(window_kernel, out_shape=(jax.ShapeDtypeStruct((rows, widt...  42.7 us
    dot_general x1, matrix products, on_device(): lax.dot_general(row_panel, window, (((0,), (0,)), ((), ())), preferred_el...  22 us
    dot_general x1, matrix products, on_device(): jnp.dot(errors, hessian_slab.astype(bf16), preferred_element_type=f32)  16.7 us
    dot_general x1, matrix products, on_device(): gate_pre = jnp.dot(token_piece, gate_weight, preferred_element_type=f32)  14.8 us
    dot_general x1, matrix products, on_device(): up_pre = jnp.dot(token_piece, up_weight, preferred_element_type=f32)  11 us
    dot_general x1, matrix products, on_device(): lax.dot_general(errors, row_panel, (((1,), (1,)), ((), ())), preferred_el...  6.42 us

profile of v1, /device:TPU:0, one launch (start us, length us, event | category | flops | bytes accessed | tf_op | source)
XLA Modules:
  0.0 242.2 jit_solution(7468534702185172492)
XLA Ops:
  1.9 16.7 %fusion.part_ref = f32[512,2048]{1,0:T(8,128)} fusion(f32[3584,2048]{1,0:T(8,128)} %param.10, f32[512,3584]{1,0:T(8,128)} %param.11), kind=kOutput, calls=%fused_computation.1 | convolution fusion | flops 7525367808 | bytes 40894464 | tf_op jit(solution)/shard_map/dot_general | solution.py:378
  18.7 0.0 slice-start
  18.7 50.9 %shard_map.86 = bf16[512,8192]{1,0:T(8,128)(2,1)} custom-call(bf16[32,4096]{1,0:T(8,128)(2,1)} %x_ref.1), custom_call_target="tpu_custom_call" | custom-call | tf_op jit(solution)/shard_map/pallas_call | solution.py:170
  69.6 0.0 copy-start.1
  69.6 0.0 slice-start.1
  69.6 0.0 slice-start.2
  69.6 0.0 slice-start.3
  69.6 14.8 %fusion.8 = f32[512,896]{1,0:T(8,128)} fusion(bf16[512,8192]{1,0:T(8,128)(2,1)} %shard_map.86, bf16[8192,896]{1,0:T(8,128)(2,1)} %param.8), kind=kOutput, calls=%fused_computation.13 | convolution fusion | flops 7516192768 | bytes 24903680 | tf_op jit(solution)/shard_map/dot_general | solution.py:379
  84.4 0.0 slice-done
  84.4 0.0 copy-done.1
  84.4 0.0 slice-done.1
  84.4 0.0 slice-done.2
  84.4 0.0 slice-done.3
  84.4 11.0 %multiply_convert_fusion.h_ref = bf16[512,896]{1,0:T(8,128)(2,1)} fusion(f32[512,896]{1,0:T(8,128)} %fusion.8, bf16[512,8192]{1,0:T(8,128)(2,1)S(1)} %copy-done.1, bf16[8192,896]{1,0:T(8,128)(2,1)S(1)} %bitcast.17), kind=kOutput, calls=%fused_computation.9 | convolution fusion | flops 7518945280 | bytes 25821184 | tf_op jit(solution)/shard_map/dot_general | solution.py:380
  95.4 66.1 %shard_map.87 = (bf16[512,3584]{1,0:T(8,128)(2,1)}, f32[7,64,2048]{2,1,0:T(8,128)}) custom-call(bf16[512,896]{1,0:T(8,128)(2,1)} %multiply_convert_fusion.h_ref, f32[512,2048]{1,0:T(8,128)} %fusion.part_ref), custom_call_target="tpu_custom_call" | custom-call | tf_op jit(solution)/shard_map/pallas_call | solution.py:266
  161.5 3.1 %reduce_sum.18 = f32[64,2048]{1,0:T(8,128)} reduce(f32[7,64,2048]{2,1,0:T(8,128)} %get-tuple-element.8, f32[]{:T(128)} %constant.35.clone.1), dimensions={0}, to_apply=%region_0.1 | reduce | flops 786432 | bytes 4194308 | tf_op jit(solution)/shard_map/reduce_sum | solution.py:384
  164.6 0.0 copy-start.2
  164.6 6.4 %fusion.3 = f32[512,512]{0,1:T(8,128)S(1)} fusion(bf16[512,3584]{1,0:T(8,128)(2,1)} %get-tuple-element.6, f32[512,3584]{1,0:T(8,128)} %param.11), kind=kOutput, calls=%fused_computation.6 | convolution fusion | flops 1880883200 | bytes 12058624 | tf_op jit(solution)/shard_map/dot_general | solution.py:396
  171.1 0.0 copy-done.2
  171.1 1.0 pad_dynamic-slice_fusion.share_ref
  172.0 42.7 %shard_map.88 = (bf16[512,2048]{1,0:T(8,128)(2,1)S(1)}, f32[7,64,512]{2,1,0:T(8,128)S(1)}) custom-call(bf16[512,2048]{1,0:T(8,128)(2,1)S(1)} %pad_dynamic-slice_fusion.share_ref, f32[512,512]{1,0:T(8,128)S(1)} %bitcast.15), custom_call_target="tpu_custom_call" | custom-call | tf_op jit(solution)/shard_map/pallas_call | solution.py:342
  214.7 0.0 copy-start
  214.8 0.9 copy-done
  215.7 1.3 reduce_sum.19
  216.9 3.3 %fusion.2 = f32[64,2048]{1,0:T(8,128)} fusion(bf16[512,2048]{1,0:T(8,128)(2,1)S(1)} %get-tuple-element.7, f32[64,2048]{1,0:T(8,128)} %reduce_sum.18, f32[512,2048]{1,0:T(8,128)} %fusion.part_ref, s32[]{:T(128)S(6)} %select_n.2, f32[]{:T(128)} %bitcast.2, f32[64,512]{1,0:T(8,128)S(1)} %reduce_sum.19, f32[512,512]{0,1:T(8,128)S(1)} %fusion.3), kind=kOutput, calls=%fused_computation.5 | convolution fusion | flops 805732352 | bytes 3933188 | tf_op jit(solution)/shard_map/dot_general | solution.py:408
  220.2 22.0 %divide_add_fusion = f32[3584,2048]{1,0:T(8,128)} fusion(f32[3584,2048]{1,0:T(8,128)} %param.10, f32[]{:T(128)} %bitcast.2, bf16[512,3584]{1,0:T(8,128)(2,1)} %get-tuple-element.6, bf16[512,2048]{1,0:T(8,128)(2,1)S(1)} %get-tuple-element.7), kind=kOutput, calls=%fused_computation | convolution fusion | flops 7530872832 | bytes 64487428 | tf_op jit(solution)/shard_map/dot_general | solution.py:404
  (1 shorter events, 0.0 us)
Async XLA Ops:
  18.7 65.7 %slice-start = ((s8[14680064]{0:T(1024)(128)(4,1)}), s8[2097152]{0:T(1024)(128)(4,1)S(1)}, s32[]{:S(2)}) async-start(s8[14680064]{0:T(1024)(128)(4,1)} %bitcast.16), calls=%async_computation | async-start | bytes 4194304
  69.6 14.8 %copy-start.1 = (bf16[512,8192]{1,0:T(8,128)(2,1)S(1)}, bf16[512,8192]{1,0:T(8,128)(2,1)}, u32[]{:S(2)}) copy-start(bf16[512,8192]{1,0:T(8,128)(2,1)} %shard_map.86) | copy-start | bytes 25165828
  69.6 14.8 %slice-start.1 = ((s8[14680064]{0:T(1024)(128)(4,1)}), s8[4194304]{0:T(1024)(128)(4,1)S(1)}, s32[]{:S(2)}) async-start(s8[14680064]{0:T(1024)(128)(4,1)} %bitcast.16), calls=%async_computation.1 | async-start | bytes 8388608
  69.6 14.8 %slice-start.2 = ((s8[14680064]{0:T(1024)(128)(4,1)}), s8[4194304]{0:T(1024)(128)(4,1)S(1)}, s32[]{:S(2)}) async-start(s8[14680064]{0:T(1024)(128)(4,1)} %bitcast.16), calls=%async_computation.2 | async-start | bytes 8388608
  69.6 14.8 %slice-start.3 = ((s8[14680064]{0:T(1024)(128)(4,1)}), s8[4194304]{0:T(1024)(128)(4,1)S(1)}, s32[]{:S(2)}) async-start(s8[14680064]{0:T(1024)(128)(4,1)} %bitcast.16), calls=%async_computation.3 | async-start | bytes 8388608
  164.6 6.4 %copy-start.2 = (bf16[512,3584]{1,0:T(8,128)(2,1)S(1)}, bf16[512,3584]{1,0:T(8,128)(2,1)}, u32[]{:S(2)}) copy-start(bf16[512,3584]{1,0:T(8,128)(2,1)} %get-tuple-element.6) | copy-start | bytes 11010052
  214.7 0.9 copy-start
